TPU v7x, 32 devices: a whole 2x2x4 slice. The times are simulated.
32 devices in a mesh: row: 4 (over y, core), col: 8 (over z, x).
Axes of the slice: x: 2, y: 2, z: 4, core: 2. Of those that a mesh axis runs over, the one named last changes fastest.
Arguments:
- kernel_panel: float32 [64, 16384], P(None, ('row', 'col')), may hold values from -4 to 16, as said below
- kernel_slab: float32 [16384, 4096], P('row', 'col'), may hold values from -4 to 20, as said below
- targets: float32 [256, 16384], P(None, ('row', 'col')), may hold values from -6 to 6
Outputs:
- updated_slab: float32 [16384, 4096], P('row', 'col')
- solved_targets: float32 [256, 16384], P('col', 'row')
- panel_factor: float32 [64, 16384], P(None, ('row', 'col'))
Inputs may be any that keep to these rules, and one draw needn't show every extreme that they name: kernel_panel[:, 0:64] is symmetric and positive definite. `kernel_slab`: rows 0 to 63 equal kernel_panel[:, 16384 - 4096 : 16384]; the last 4096 rows form a symmetric matrix.
All inputs are finite; a program needn't handle non-finite values.
Results may differ from a plain program's by a relative error of at most 0.00018.
Values sent between devices are 32-bit elements; how exact they have to be, the bound alone decides.
A program may use at most 64 MiB of HBM per device.

v0:
```python
import jax
import jax.numpy as jnp
from jax import lax
from jax.sharding import PartitionSpec as P


def spread(block, axis, source):
    block = jnp.where(lax.axis_index(axis) == source, block, jnp.zeros_like(block))
    return lax.psum(block, axis)


def lower_solve(factor, values):
    return jax.scipy.linalg.solve_triangular(factor, values, lower=True)


def body(kernel_panel, kernel_slab, targets):
    highest = lax.Precision.HIGHEST
    panel_width = kernel_panel.shape[0]
    row_count = lax.axis_size("row")
    row_index = lax.axis_index("row")
    flat_index = lax.axis_index(("row", "col"))
    corner_rows = jnp.concatenate([kernel_panel[:, :panel_width], targets[:, :panel_width]], 0)
    shared = spread(corner_rows, ("row", "col"), 0)
    lower_factor = jnp.linalg.cholesky(shared[:panel_width])
    panel_factor = lower_solve(lower_factor, kernel_panel)
    gathered = lax.all_gather(panel_factor, "col", axis=1, tiled=True)
    slab_factor = spread(panel_factor, "row", row_count - 1)
    product = lax.dot_general(
        gathered,
        slab_factor,
        (((0,), (0,)), ((), ())),
        precision=highest,
        preferred_element_type=jnp.float32,
    )
    update = kernel_slab - product
    head_rows = jnp.where(row_index == 0, slab_factor, update[:panel_width])
    updated_slab = jnp.concatenate([head_rows, update[panel_width:]], 0)
    solved_lead = lower_solve(lower_factor, shared[panel_width:].T).T
    result = targets - jnp.dot(
        solved_lead, panel_factor, precision=highest, preferred_element_type=jnp.float32
    )
    head_cols = jnp.where(flat_index == 0, solved_lead, result[:, :panel_width])
    result = jnp.concatenate([head_cols, result[:, panel_width:]], 1)
    solved_targets = lax.all_to_all(result, "col", split_axis=0, concat_axis=1, tiled=True)
    return (updated_slab, solved_targets, panel_factor)


def solution(mesh):
    in_specs = (P(None, ("row", "col")), P("row", "col"), P(None, ("row", "col")))
    out_specs = (P("row", "col"), P("col", "row"), P(None, ("row", "col")))
    return jax.shard_map(body, mesh=mesh, in_specs=in_specs, out_specs=out_specs, check_vma=False)
```

profile of v0, /device:TPU:0, one launch (start us, length us, event | category | flops | bytes accessed | tf_op | source)
XLA Modules:
  0.0 250.5 jit_solution(13872501466629735246)
XLA Ops:
  7.2 0.0 all-reduce.3.cloned.1.call-start
  7.2 0.8 slice.42
  8.0 0.1 copy.26
  8.1 1.2 copy.19
  9.3 0.7 maximum_select_fusion
  10.1 0.0 all-reduce.3.cloned.1.call-update
  10.1 0.0 all-reduce.5.cloned.1.call-start
  10.1 127.3 %all-reduce.3.cloned.1.call-done = f32[320,64]{0,1:T(8,128)} async-done(((f32[320,64]{0,1:T(8,128)}), f32[320,64]{0,1:T(8,128)}) %all-reduce.3.cloned.1.call-update) | async-done | bytes 81936 | tf_op jit(solution)/shard_map/psum | solution.py:9
  137.5 0.8 slice.51
  138.2 0.1 copy.20
  138.3 0.8 fusion.6
  139.1 5.8 %cholesky.16 = f32[64,64]{1,0:T(8,128)S(1)} custom-call(f32[64,64]{1,0:T(8,128)S(1)} %fusion.6), custom_call_target="Cholesky" | custom-call | tf_op jit(solution)/shard_map/jit(cholesky)/cholesky | solution.py:24
  145.0 0.6 compare_reduce_fusion
  145.6 0.7 fusion.2
  146.3 4.9 %custom-call.10 = f32[1,64,64]{1,2,0:T(8,128)S(1)} custom-call(f32[1,64,64]{2,1,0:T(8,128)S(1)} %fusion.2), custom_call_target="InvertDiagBlocksLowerTriangular" | custom-call | tf_op jit(solution)/shard_map/jit(_solve_triangular)/triangular_solve | solution.py:13
  151.2 1.9 broadcast_select_fusion
  153.1 0.0 all-reduce.5.cloned.1.call-update
  153.1 0.0 all-gather.2.cloned.1.call-start
  153.2 0.7 all-gather.2.cloned.1.call-update
  153.9 1.2 fusion
  155.1 1.5 convolution_subtract_fusion.1
  156.7 1.0 copy.23
  157.7 6.3 %all-to-all-start = ((f32[8,32,512]{2,1,0:T(8,128)}), f32[8,32,512]{2,1,0:T(8,128)S(1)}, u32[]{:S(2)}, u32[]{:S(2)}) async-start(f32[8,32,512]{2,1,0:T(8,128)} %bitcast.4), calls=%async_computation | async-start | bytes 1048576 | tf_op jit(solution)/shard_map/all_to_all | solution.py:44
  164.0 12.9 %all-to-all-done = f32[8,32,512]{2,1,0:T(8,128)S(1)} async-done(((f32[8,32,512]{2,1,0:T(8,128)}), f32[8,32,512]{2,1,0:T(8,128)S(1)}, u32[]{:S(2)}, u32[]{:S(2)}) %all-to-all-start) | async-done | bytes 524320 | tf_op jit(solution)/shard_map/all_to_all | solution.py:44
  176.9 0.8 copy.27
  177.8 7.7 %all-reduce.5.cloned.1.call-done = f32[64,512]{1,0:T(8,128)} async-done(((f32[64,512]{1,0:T(8,128)}), f32[64,512]{1,0:T(8,128)}) %all-reduce.5.cloned.1.call-update) | async-done | bytes 131088 | tf_op jit(solution)/shard_map/psum | solution.py:9
  185.5 43.2 %all-gather.2.cloned.1.call-done = f32[64,4096]{1,0:T(8,128)} async-done(((f32[64,512]{1,0:T(8,128)}), f32[64,4096]{1,0:T(8,128)}) %all-gather.2.cloned.1.call-update) | async-done | bytes 1048592 | tf_op jit(solution)/shard_map/all_gather | solution.py:26
  228.8 9.8 %convolution_subtract_fusion = f32[4096,512]{1,0:T(8,128)S(1)} fusion(f32[4096,512]{1,0:T(8,128)} %param.4, f32[64,4096]{1,0:T(8,128)} %all-gather.2.cloned.1.call-done, f32[64,512]{1,0:T(8,128)} %all-reduce.5.cloned.1.call-done), kind=kOutput, calls=%fused_computation.1 | convolution fusion | flops 1612709888 | bytes 17956864 | tf_op jit(solution)/shard_map/dot_general | solution.py:28
  238.5 0.0 copy-start
  238.5 1.0 slice.53
  239.5 0.0 copy-done
  239.5 4.4 %pad_maximum_fusion = f32[4096,512]{1,0:T(8,128)} fusion(f32[4032,512]{1,0:T(8,128)S(1)} %slice.53, f32[64,512]{1,0:T(8,128)S(1)} %slice_select_fusion), kind=kLoop, calls=%fused_computation | loop fusion | flops 2097152 | bytes 16777216 | tf_op jit(solution)/shard_map/concatenate | solution.py:37
  (6 shorter events, 0.1 us)
Async XLA Ops:
  7.2 130.3 %all-reduce.3.cloned.1.call-start = ((), (), s32[]{:S(2)}) async-start(), calls=%async_computation.1 | async-start | bytes 196608 | tf_op jit(solution)/shard_map/psum | solution.py:9
  10.1 175.4 %all-reduce.5.cloned.1.call-start = ((), (), s32[]{:S(2)}) async-start(), calls=%async_computation.2 | async-start | bytes 262144 | tf_op jit(solution)/shard_map/psum | solution.py:9
  153.1 75.6 %all-gather.2.cloned.1.call-start = ((), (), s32[]{:S(2)}) async-start(), calls=%async_computation.3 | async-start | bytes 1179648 | tf_op jit(solution)/shard_map/all_gather | solution.py:26
  157.7 19.3 %all-to-all-start = ((f32[8,32,512]{2,1,0:T(8,128)}), f32[8,32,512]{2,1,0:T(8,128)S(1)}, u32[]{:S(2)}, u32[]{:S(2)}) async-start(f32[8,32,512]{2,1,0:T(8,128)} %bitcast.4), calls=%async_computation | async-start | bytes 1048576 | tf_op jit(solution)/shard_map/all_to_all | solution.py:44
  238.5 1.0 copy-start
Sparse Core Ops, SparseCore 0:
  14.2 123.2 all-reduce.2
  153.3 32.2 all-reduce.4
  188.5 40.1 all-gather.1
where the time goes:
time: 251 us; the launch traced here: 250 us
  waiting for transfers between devices  192 us (76%)
  other arithmetic  18 us (7%)
  matrix products  14.4 us (6%)
  between operations  13.9 us (6%)
  starting transfers between devices  6.44 us (3%)
  local copies, waits for them, and re-layouts  5.76 us (2%)
    psum x2, waiting for transfers between devices, spread(): return lax.psum(block, axis)  135 us
    all_gather x1, waiting for transfers between devices, body(): gathered = lax.all_gather(panel_factor, 'col', axis=1, tiled=True)  43.2 us
    all_to_all x1, waiting for transfers between devices, body(): lax.all_to_all(result, 'col', split_axis=0, concat_axis=1, tiled=True)  12.9 us
    dot_general x1, matrix products, body(): lax.dot_general(gathered, slab_factor, (((0,), (0,)), ((), ())), precisio...  9.76 us
    another operation x3, other arithmetic, body(): lower_factor = jnp.linalg.cholesky(shared[:panel_width])  6.52 us
    all_to_all x1, starting transfers between devices, body(): lax.all_to_all(result, 'col', split_axis=0, concat_axis=1, tiled=True)  6.32 us
    another operation x2, other arithmetic, lower_solve(): return jax.scipy.linalg.solve_triangular(factor, values, lower=True)  5.55 us
  transfers between devices with their start and end apart: 4, of which 4 were waited for; matrix products, arithmetic and copies ran while one was open for 2% of the time, Pallas kernels for 0%

commit v1 on v0

v1 whole, which is shorter than its diff:
```python
import functools

import jax
import jax.numpy as jnp
from jax import lax
from jax.experimental import pallas as pl
from jax.experimental.pallas import tpu as pltpu
from jax.sharding import PartitionSpec as P

MESH = pl.DeviceIdType.MESH
HIGHEST = lax.Precision.HIGHEST
Z_SIZE = 4


def dot(a, b, dims=((1,), (0,)), precision=None):
    return lax.dot_general(a, b, (dims, ((), ())), precision=precision, preferred_element_type=jnp.float32)


def split3(value):
    high = value.astype(jnp.bfloat16)
    rest = value - high.astype(jnp.float32)
    mid = rest.astype(jnp.bfloat16)
    low = (rest - mid.astype(jnp.float32)).astype(jnp.bfloat16)
    return high, mid, low


def inverse_factor(corner):
    size = corner.shape[0]
    rows = lax.broadcasted_iota(jnp.int32, corner.shape, 0)
    lanes = lax.broadcasted_iota(jnp.int32, corner.shape, 1)
    work = jnp.where(lanes < size, corner, jnp.where(lanes == rows + size, 1.0, 0.0))
    for j in range(size):
        pivot = work[j : j + 1, :]
        scaled = pivot * (1.0 / work[j : j + 1, j : j + 1])
        work = work - jnp.where(rows > j, work[:, j : j + 1], 0.0) * scaled
    diagonal = jnp.sum(jnp.where(lanes == rows, work, 0.0), axis=1, keepdims=True)
    return work * (1.0 / jnp.sqrt(diagonal))


def kernel(
    rows_n, cols_n, k_ref, lead_ref, t_ref, s_ref, us_ref, st_ref, pf_ref,
    gp, tg, ks, note, notes, xtp, rhs, yp,
    slab_sem, own_sem, up_sem, down_sem, side_sem, panel_sem, t_send, t_recv, ks_send, ks_recv,
    note_send, note_fwd, note_recv,
):
    row, col = lax.axis_index("row"), lax.axis_index("col")
    size, blk = k_ref.shape
    tgt = tg.shape[1]
    zn = Z_SIZE
    xn = cols_n // zn
    z, x = col // xn, col % xn
    last = rows_n - 1

    def remote(src, dst, send, recv, where):
        return pltpu.make_async_remote_copy(
            src_ref=src, dst_ref=dst, send_sem=send, recv_sem=recv, device_id=where, device_id_type=MESH
        )

    def slab_copy(b):
        part = pl.ds(pl.multiple_of(b * blk, blk), blk)
        return pltpu.make_async_copy(s_ref.at[part], us_ref.at[part], slab_sem.at[b])

    own_target = pltpu.make_async_copy(
        t_ref.at[pl.ds(pl.multiple_of(col * tgt, tgt), tgt)], tg.at[col], own_sem
    )

    barrier = pltpu.get_barrier_semaphore()
    for step in range(1, cols_n):
        pl.semaphore_signal(barrier, inc=1, device_id=(row, lax.rem(col + step, cols_n)), device_id_type=MESH)
    for step in range(1, rows_n):
        pl.semaphore_signal(barrier, inc=1, device_id=(lax.rem(row + step, rows_n), col), device_id_type=MESH)
    own_target.start()
    for b in range(cols_n):
        slab_copy(b).start()
    gp[col] = k_ref[...]
    pl.semaphore_wait(barrier, cols_n - 1 + rows_n - 1)

    def up(zo):
        o = zo * xn + x
        return remote(gp.at[o], gp.at[o], up_sem.at[zo], panel_sem.at[o], (row, col + xn))

    def down(zo):
        o = zo * xn + x
        return remote(gp.at[o], gp.at[o], down_sem.at[zo], panel_sem.at[o], (row, col - xn))

    def side(zo, step):
        o = zo * xn + x
        peer = z * xn + lax.rem(x + step, xn)
        return remote(gp.at[o], gp.at[o], side_sem.at[zo, step - 1], panel_sem.at[o], (row, peer))

    def slab_panel(step):
        return remote(k_ref, ks, ks_send.at[step - 1], ks_recv, (lax.rem(row + step, rows_n), col))

    def target(step):
        peer = lax.rem(col + step, cols_n)
        return remote(
            t_ref.at[pl.ds(pl.multiple_of(peer * tgt, tgt), tgt)], tg.at[col],
            t_send.at[step - 1], t_recv.at[col], (row, peer),
        )

    def note_out(c):
        return remote(notes.at[c], note, note_send.at[c], note_recv, (row, c))

    def note_on(step):
        return remote(note, note, note_fwd.at[step - 1], note_recv, (lax.rem(row + step, rows_n), col))

    @pl.when(z + 1 < zn)
    def _():
        up(z).start()

    @pl.when(z > 0)
    def _():
        down(z).start()

    for step in range(1, xn):
        side(z, step).start()

    @pl.when(row == last)
    def _():
        for step in range(1, rows_n):
            slab_panel(step).start()

    for step in range(1, cols_n):
        target(step).start()

    @pl.when((row == 0) & (col == 0))
    def _():
        done = inverse_factor(k_ref[:, : 2 * size])
        lanes = lax.broadcasted_iota(jnp.int32, done.shape, 1)
        for c in range(cols_n):
            lead = lead_ref[c * tgt : (c + 1) * tgt, :]
            notes[c] = done
            notes[c, :tgt, :] = jnp.where(lanes[:tgt] < size, lead, done[:tgt])
        note[...] = notes[0]
        for c in range(1, cols_n):
            note_out(c).start()

    for d in range(1, zn):
        @pl.when(z - d >= 0)
        def _():
            up(z - d).wait_recv()

            @pl.when(z + 1 < zn)
            def _():
                up(z - d).start()

            for step in range(1, xn):
                side(z - d, step).start()

        @pl.when(z + d < zn)
        def _():
            down(z + d).wait_recv()

            @pl.when(z > 0)
            def _():
                down(z + d).start()

            for step in range(1, xn):
                side(z + d, step).start()

    @pl.when((row > 0) | (col > 0))
    def _():
        remote(note, note, note_fwd.at[0], note_recv, (row, col)).wait_recv()

    @pl.when(row == 0)
    def _():
        for step in range(1, rows_n):
            note_on(step).start()

    @pl.when(row == last)
    def _():
        ks[...] = k_ref[...]

    @pl.when(row != last)
    def _():
        remote(k_ref, ks, ks_send.at[0], ks_recv, (row, col)).wait_recv()

    inverse = note[:, size:]
    wide = jnp.concatenate([note[...]] * 4, axis=0).T[size:, :]
    high, mid, low = split3(wide)
    rhs[...] = jnp.concatenate([high, mid, low, high, mid, high], axis=0)
    pf_ref[...] = dot(inverse, k_ref[...], precision=HIGHEST)
    slab_factor = dot(inverse, ks[...], precision=HIGHEST)
    high, mid, _ = split3(slab_factor)
    yp[...] = jnp.concatenate([high, mid, high, mid], axis=0)

    for step in range(1, xn):
        for zo in range(zn):
            o = zo * xn + lax.rem(x + step, xn)
            remote(gp.at[o], gp.at[o], side_sem.at[0, 0], panel_sem.at[o], (row, col)).wait_recv()

    lanes4 = lax.broadcasted_iota(jnp.int32, (blk, 4 * size), 1)

    def slab_step(b, carry):
        high, mid, low = split3(gp[b])
        lhs = jnp.concatenate([high, high, high, mid, mid, low], axis=0)
        xt = dot(lhs, rhs[...], dims=((0,), (0,)))
        rest = xt - xt.astype(jnp.bfloat16).astype(jnp.float32)
        packed = jnp.where(lanes4 < 2 * size, xt, rest).astype(jnp.bfloat16)
        xtp[b] = packed
        product = dot(packed, yp[...])
        slab_copy(b).wait()
        part = pl.ds(pl.multiple_of(b * blk, blk), blk)
        us_ref[part, :] = us_ref[part, :] - product
        return carry

    lax.fori_loop(0, cols_n, slab_step, 0)

    @pl.when(row == 0)
    def _():
        us_ref[:size, :] = slab_factor

    solved = dot(note[:tgt, :size], wide, precision=HIGHEST)
    lanes = lax.broadcasted_iota(jnp.int32, solved.shape, 1)
    rest = solved - solved.astype(jnp.bfloat16).astype(jnp.float32)
    zp = jnp.where(lax.rem(lanes, 2 * size) < size, solved, rest).astype(jnp.bfloat16)

    own_target.wait()
    for step in range(1, cols_n):
        o = lax.rem(col + step, cols_n)
        remote(t_ref.at[pl.ds(0, tgt)], tg.at[o], t_send.at[0], t_recv.at[o], (row, col)).wait_recv()

    def target_step(b, carry):
        part = pl.ds(pl.multiple_of(b * blk, blk), blk)
        st_ref[:, part] = tg[b] - dot(zp, xtp[b], dims=((1,), (1,)))
        return carry

    lax.fori_loop(0, cols_n, target_step, 0)

    @pl.when(row == 0)
    def _():
        pair = slice(0, 2 * size)
        st_ref[:, pair] = jnp.where(lanes[:, pair] < size, solved[:, pair], st_ref[:, pair])

    for zo in range(zn):
        @pl.when((z >= zo) & (z + 1 < zn))
        def _():
            up(zo).wait_send()

        @pl.when((z <= zo) & (z > 0))
        def _():
            down(zo).wait_send()

        for step in range(1, xn):
            side(zo, step).wait_send()

    for step in range(1, cols_n):
        target(step).wait_send()

    @pl.when(row == last)
    def _():
        for step in range(1, rows_n):
            slab_panel(step).wait_send()

    @pl.when((row == 0) & (col == 0))
    def _():
        for c in range(1, cols_n):
            note_out(c).wait_send()

    @pl.when(row == 0)
    def _():
        for step in range(1, rows_n):
            note_on(step).wait_send()


def body(rows_n, cols_n, kernel_panel, kernel_slab, targets):
    size, blk = kernel_panel.shape
    rows, _ = kernel_slab.shape
    tgt = targets.shape[0] // cols_n
    xn = cols_n // Z_SIZE
    f32 = jnp.float32
    vmem = pl.BlockSpec(memory_space=pltpu.VMEM)
    hbm = pl.BlockSpec(memory_space=pl.ANY)
    dma = pltpu.SemaphoreType.DMA
    us, st, pf = pl.pallas_call(
        functools.partial(kernel, rows_n, cols_n),
        out_shape=OUT((rows, blk), (tgt, rows), (size, blk)),
        in_specs=[vmem, vmem, hbm, hbm],
        out_specs=[vmem] * 3,
        scratch_shapes=[
            pltpu.VMEM((cols_n, size, blk), f32),
            pltpu.VMEM((cols_n, tgt, blk), f32),
            pltpu.VMEM((size, blk), f32),
            pltpu.VMEM((size, 2 * size), f32),
            pltpu.VMEM((cols_n, size, 2 * size), f32),
            pltpu.VMEM((cols_n, blk, 4 * size), jnp.bfloat16),
            pltpu.VMEM((6 * size, 4 * size), jnp.bfloat16),
            pltpu.VMEM((4 * size, blk), jnp.bfloat16),
            dma((cols_n,)), dma, dma((Z_SIZE,)), dma((Z_SIZE,)), dma((Z_SIZE, xn - 1)), dma((cols_n,)),
            dma((cols_n - 1,)), dma((cols_n,)), dma((rows_n - 1,)), dma,
            dma((cols_n,)), dma((rows_n - 1,)), dma,
        ],
        compiler_params=pltpu.CompilerParams(
            collective_id=0, has_side_effects=True, vmem_limit_bytes=36 * 1024 * 1024
        ),
        cost_estimate=pl.CostEstimate(
            flops=2 * rows * blk * 4 * size, bytes_accessed=8 * rows * blk, transcendentals=0
        ),
    )(kernel_panel, targets[:, : 2 * size], targets, kernel_slab)
    return us, st, pf


def OUT(*shapes):
    return [pltpu.VMEM(shape, jnp.float32) for shape in shapes]


def solution(mesh):
    in_specs = (P(None, ("row", "col")), P("row", "col"), P(None, ("row", "col")))
    out_specs = (P("row", "col"), P("col", "row"), P(None, ("row", "col")))
    step = functools.partial(body, mesh.shape["row"], mesh.shape["col"])
    return jax.shard_map(step, mesh=mesh, in_specs=in_specs, out_specs=out_specs, check_vma=False)
```

time: 251 us -> 52.4 us (0.21)
  waiting for transfers between devices: 192 us -> 0 us
  Pallas kernels: 0 us -> 40.4 us
  other arithmetic: 18 us -> 0 us
  matrix products: 14.4 us -> 0 us
  between operations: 13.9 us -> 0.65 us
  starting transfers between devices: 6.44 us -> 0 us
  local copies, waits for them, and re-layouts: 5.76 us -> 11.1 us
    psum x2 -> x0, waiting for transfers between devices: 135 us -> none  [spread(): return lax.psum(block, axis)]
    all_gather x1 -> x0, waiting for transfers between devices: 43.2 us -> none  [body(): gathered = lax.all_gather(panel_factor, 'col', axis=1, tiled=True)]
    pallas_call x0 -> x1, Pallas kernels: none -> 40.4 us  [body(): pl.pallas_call(functools.partial(kernel, rows_n, cols_n), out_shape=OUT((...]
    all_to_all x1 -> x0, waiting for transfers between devices: 12.9 us -> none  [body(): lax.all_to_all(result, 'col', split_axis=0, concat_axis=1, tiled=True)]
    another operation x5 -> x0, other arithmetic: 12.1 us -> none  [the longest x3 6.52 us: body(): lower_factor = jnp.linalg.cholesky(shared[:panel_width])]
    dot_general x2 -> x0, matrix products: 11.3 us -> none  [the longest x1 9.76 us: body(): lax.dot_general(gathered, slab_factor, (((0,), (0,)), ((), ())), precisio...]
    unnamed x4 -> x9, local copies, waits for them, and re-layouts: 1.33 us -> 10.2 us
    all_to_all x1 -> x0, starting transfers between devices: 6.32 us -> none  [body(): lax.all_to_all(result, 'col', split_axis=0, concat_axis=1, tiled=True)]
  transfers between devices with their start and end apart: 4 -> 0, of which waited for: 4 -> 0; matrix products, arithmetic and copies ran while one was open for 2% -> 0% of each run, Pallas kernels for 0% -> 0%
where the time goes in v1:
time: 52.4 us; the launch traced here: 52.1 us
  Pallas kernels  40.4 us (77%)
  local copies, waits for them, and re-layouts  11.1 us (21%)
  between operations  0.65 us (1%)
    pallas_call x1, Pallas kernels, body(): pl.pallas_call(functools.partial(kernel, rows_n, cols_n), out_shape=OUT((...  40.4 us
    unnamed x9, local copies, waits for them, and re-layouts  10.2 us

profile of v1, /device:TPU:0, one launch (start us, length us, event | category | flops | bytes accessed | tf_op | source)
XLA Modules:
  0.0 52.1 jit_solution(994884867040749377)
XLA Ops:
  0.6 0.9 %slice.3.lead_ref = f32[256,128]{1,0:T(8,128)S(1)} slice(f32[256,512]{1,0:T(8,128)} %t_ref.1), slice={[0:256], [0:128]} | slice | bytes 262144 | tf_op jit(solution)/shard_map/slice | solution.py:299
  1.5 0.0 copy-start
  1.6 3.4 %copy-done = f32[4096,512]{1,0:T(8,128)S(1)} copy-done((f32[4096,512]{1,0:T(8,128)S(1)}, f32[4096,512]{1,0:T(8,128)}, u32[]{:S(2)}) %copy-start) | copy-done | bytes 8388632
  4.9 0.0 copy-start.1
  4.9 1.0 %copy-done.1 = f32[256,512]{1,0:T(8,128)S(1)} copy-done((f32[256,512]{1,0:T(8,128)S(1)}, f32[256,512]{1,0:T(8,128)}, u32[]{:S(2)}) %copy-start.1) | copy-done | bytes 524312
  6.0 0.0 copy-start.2
  6.0 0.9 %copy-done.2 = f32[64,512]{1,0:T(8,128)S(1)} copy-done((f32[64,512]{1,0:T(8,128)S(1)}, f32[64,512]{1,0:T(8,128)}, u32[]{:S(2)}) %copy-start.2) | copy-done | bytes 131096
  6.9 40.4 %shard_map.58 = (f32[4096,512]{1,0:T(8,128)S(1)}, f32[32,4096]{1,0:T(8,128)S(1)}, f32[64,512]{1,0:T(8,128)S(1)}) custom-call(f32[64,512]{1,0:T(8,128)S(1)} %copy-done.2, f32[256,128]{1,0:T(8,128)S(1)} %slice.3.lead_ref, f32[256,512]{1,0:T(8,128)S(1)} %copy-done.1, f32[4096,512]{1,0:T(8,128)S(1)} %copy-done), custom_call_target="tpu_custom_call" | custom-call | flops 1073741824 | bytes 16777216 | tf_op jit(solution)/shard_map/pallas_call | solution.py:275
  47.3 3.4 %copy.9 = f32[4096,512]{1,0:T(8,128)} copy(f32[4096,512]{1,0:T(8,128)S(1)} %get-tuple-element.3) | data formatting | bytes 16777216
  50.7 0.7 %copy.11 = f32[64,512]{1,0:T(8,128)} copy(f32[64,512]{1,0:T(8,128)S(1)} %get-tuple-element.5) | data formatting | bytes 262144
  51.3 0.8 %copy.10 = f32[32,4096]{1,0:T(8,128)} copy(f32[32,4096]{1,0:T(8,128)S(1)} %get-tuple-element.4) | data formatting | bytes 1048576
Async XLA Ops:
  1.5 3.4 %copy-start = (f32[4096,512]{1,0:T(8,128)S(1)}, f32[4096,512]{1,0:T(8,128)}, u32[]{:S(2)}) copy-start(f32[4096,512]{1,0:T(8,128)} %s_ref.1) | copy-start | bytes 25165828
  4.9 1.0 %copy-start.1 = (f32[256,512]{1,0:T(8,128)S(1)}, f32[256,512]{1,0:T(8,128)}, u32[]{:S(2)}) copy-start(f32[256,512]{1,0:T(8,128)} %t_ref.1) | copy-start | bytes 1572868
  6.0 0.9 %copy-start.2 = (f32[64,512]{1,0:T(8,128)S(1)}, f32[64,512]{1,0:T(8,128)}, u32[]{:S(2)}) copy-start(f32[64,512]{1,0:T(8,128)} %k_ref.1) | copy-start | bytes 393220

commit v2 on v1

v2 whole, which is shorter than its diff:
```python
import functools

import jax
import jax.numpy as jnp
from jax import lax
from jax.experimental import pallas as pl
from jax.experimental.pallas import tpu as pltpu
from jax.sharding import PartitionSpec as P

MESH = pl.DeviceIdType.MESH
HIGHEST = lax.Precision.HIGHEST
Z_SIZE = 4


def dot(a, b, dims=((1,), (0,)), precision=None):
    return lax.dot_general(a, b, (dims, ((), ())), precision=precision, preferred_element_type=jnp.float32)


def split3(value):
    high = value.astype(jnp.bfloat16)
    rest = value - high.astype(jnp.float32)
    mid = rest.astype(jnp.bfloat16)
    low = (rest - mid.astype(jnp.float32)).astype(jnp.bfloat16)
    return high, mid, low


def eliminate_pair(work, j):
    rows = lax.broadcasted_iota(jnp.int32, work.shape, 0)
    first, second = work[j : j + 1, :], work[j + 1 : j + 2, :]
    cross = work[j + 1 : j + 2, j : j + 1]
    scale = 1.0 / work[j : j + 1, j : j + 1]
    ratio = cross * scale
    below = second - ratio * first
    other = 1.0 / (work[j + 1 : j + 2, j + 1 : j + 2] - ratio * cross)
    second_part = below * other
    first_part = first * scale - ratio * second_part
    change = work[:, j : j + 1] * first_part + work[:, j + 1 : j + 2] * second_part
    return jnp.where(rows > j + 1, work - change, jnp.where(rows == j + 1, below, work))


def kernel(
    rows_n, cols_n, k_ref, t_ref, s_ref,
    us_ref, tg, xtp, pf_ref, zp_ref, z_ref, sel_ref,
    gp, ks, note, notes, lead, lhs, rhs, yp,
    slab_sem, own_sem, up_sem, down_sem, side_sem, panel_sem, t_send, t_recv, ks_send, ks_recv,
    note_send, note_fwd, note_recv,
):
    row, col = lax.axis_index("row"), lax.axis_index("col")
    size, blk = k_ref.shape
    tgt = tg.shape[1]
    zn = Z_SIZE
    xn = cols_n // zn
    z, x = col // xn, col % xn
    last = rows_n - 1
    first_device = (row == 0) & (col == 0)

    def remote(src, dst, send, recv, where):
        return pltpu.make_async_remote_copy(
            src_ref=src, dst_ref=dst, send_sem=send, recv_sem=recv, device_id=where, device_id_type=MESH
        )

    def slab_copy(b):
        part = pl.ds(pl.multiple_of(b * blk, blk), blk)
        return pltpu.make_async_copy(s_ref.at[part], us_ref.at[part], slab_sem.at[b])

    own_panel = pltpu.make_async_copy(k_ref, gp.at[col], own_sem.at[0])
    own_target = pltpu.make_async_copy(
        t_ref.at[pl.ds(pl.multiple_of(col * tgt, tgt), tgt)], tg.at[col], own_sem.at[1]
    )
    own_lead = pltpu.make_async_copy(t_ref.at[:, pl.ds(0, 2 * size)], lead, own_sem.at[2])

    barrier = pltpu.get_barrier_semaphore()
    for step in range(1, cols_n):
        pl.semaphore_signal(barrier, inc=1, device_id=(row, lax.rem(col + step, cols_n)), device_id_type=MESH)
    for step in range(1, rows_n):
        pl.semaphore_signal(barrier, inc=1, device_id=(lax.rem(row + step, rows_n), col), device_id_type=MESH)
    own_panel.start()
    own_target.start()

    @pl.when(first_device)
    def _():
        own_lead.start()

    for b in range(cols_n):
        slab_copy(b).start()
    own_panel.wait()
    pl.semaphore_wait(barrier, cols_n - 1 + rows_n - 1)

    def up(zo):
        o = zo * xn + x
        return remote(gp.at[o], gp.at[o], up_sem.at[zo], panel_sem.at[o], (row, col + xn))

    def down(zo):
        o = zo * xn + x
        return remote(gp.at[o], gp.at[o], down_sem.at[zo], panel_sem.at[o], (row, col - xn))

    def side(zo, step):
        o = zo * xn + x
        peer = z * xn + lax.rem(x + step, xn)
        return remote(gp.at[o], gp.at[o], side_sem.at[zo, step - 1], panel_sem.at[o], (row, peer))

    def slab_panel(step):
        return remote(gp.at[col], ks, ks_send.at[step - 1], ks_recv, (lax.rem(row + step, rows_n), col))

    def target(step):
        peer = lax.rem(col + step, cols_n)
        return remote(
            t_ref.at[pl.ds(pl.multiple_of(peer * tgt, tgt), tgt)], tg.at[col],
            t_send.at[step - 1], t_recv.at[col], (row, peer),
        )

    def note_out(c):
        return remote(notes.at[c], note, note_send.at[c], note_recv, (row, c))

    def note_on(step):
        return remote(note, note, note_fwd.at[step - 1], note_recv, (lax.rem(row + step, rows_n), col))

    half = lax.broadcasted_iota(jnp.int32, (blk, 2 * size), 1) < size

    def prepare(o):
        block = gp[o]
        turned = jnp.concatenate([block, block], axis=0).T
        high = turned.astype(jnp.bfloat16).astype(jnp.float32)
        rest = turned - high
        mid = rest.astype(jnp.bfloat16).astype(jnp.float32)
        pair = jnp.where(half, high, mid).astype(jnp.bfloat16)
        other = jnp.where(half, rest - mid, high).astype(jnp.bfloat16)
        lhs[o] = jnp.concatenate([pair, other], axis=1)

    def pass_up(d):
        up(z - d).wait_recv()

        @pl.when(z + 1 < zn)
        def _():
            up(z - d).start()

        for step in range(1, xn):
            side(z - d, step).start()

    def pass_down(d):
        down(z + d).wait_recv()

        @pl.when(z > 0)
        def _():
            down(z + d).start()

        for step in range(1, xn):
            side(z + d, step).start()

    @pl.when(z + 1 < zn)
    def _():
        up(z).start()

    @pl.when(z > 0)
    def _():
        down(z).start()

    for step in range(1, xn):
        side(z, step).start()

    @pl.when(row == last)
    def _():
        for step in range(1, rows_n):
            slab_panel(step).start()

    for step in range(1, cols_n):
        target(step).start()

    @pl.when(first_device)
    def _():
        corner = gp[0, :, : 2 * size]
        rows = lax.broadcasted_iota(jnp.int32, corner.shape, 0)
        lanes = lax.broadcasted_iota(jnp.int32, corner.shape, 1)
        work = jnp.where(lanes < size, corner, jnp.where(lanes == rows + size, 1.0, 0.0))
        for j in range(0, size, 2):
            work = eliminate_pair(work, j)
            if j == size // 2:
                pass_down(1)
            if j == 3 * size // 4:
                pass_down(2)
        diagonal = jnp.sum(jnp.where(lanes == rows, work, 0.0), axis=1, keepdims=True)
        done = work * (1.0 / jnp.sqrt(diagonal))
        own_lead.wait()
        for c in range(cols_n):
            notes[c] = done
            notes[c, :tgt, :] = jnp.where(lanes[:tgt] < size, lead[c * tgt : (c + 1) * tgt, :], done[:tgt])
        for c in range(1, cols_n):
            note_out(c).start()
        note[...] = notes[0]
        for step in range(1, rows_n):
            note_on(step).start()
        pass_down(3)
        prepare(col)
        for d in range(1, zn):
            prepare(col + d * xn)

    @pl.when(jnp.logical_not(first_device))
    def _():
        prepare(col)
        for d in range(1, zn):
            @pl.when(z - d >= 0)
            def _():
                pass_up(d)
                prepare(col - d * xn)

            @pl.when(z + d < zn)
            def _():
                pass_down(d)
                prepare(col + d * xn)

        remote(note, note, note_fwd.at[0], note_recv, (row, col)).wait_recv()

        @pl.when(row == 0)
        def _():
            for step in range(1, rows_n):
                note_on(step).start()

    @pl.when(row == last)
    def _():
        ks[...] = gp[col]

    @pl.when(row != last)
    def _():
        remote(gp.at[col], ks, ks_send.at[0], ks_recv, (row, col)).wait_recv()

    inverse = note[:, size:]
    wide = jnp.concatenate([note[...]] * 4, axis=0).T[size:, :]
    high, mid, low = split3(wide)
    rhs[...] = jnp.concatenate([high, high, high, mid, low, mid], axis=0)
    pf_ref[...] = dot(inverse, gp[col], precision=HIGHEST)
    slab_factor = dot(inverse, ks[...], precision=HIGHEST)
    high, mid, _ = split3(slab_factor)
    yp[...] = jnp.concatenate([high, mid, high, mid], axis=0)
    solved = dot(note[:tgt, :size], wide, precision=HIGHEST)
    lanes = lax.broadcasted_iota(jnp.int32, solved.shape, 1)
    rest = solved - solved.astype(jnp.bfloat16).astype(jnp.float32)
    zp_ref[...] = jnp.where(lax.rem(lanes, 2 * size) < size, solved, rest).astype(jnp.bfloat16)
    z_ref[...] = solved[:, : 2 * size]
    sel_ref[...] = jnp.where((lanes[:, : 2 * size] < size) & (row == 0), 1.0, 0.0)

    lanes4 = lax.broadcasted_iota(jnp.int32, (blk, 4 * size), 1)

    def update(b):
        xt = dot(lhs[b], rhs[: 4 * size]) + dot(lhs[b, :, : 2 * size], rhs[4 * size :])
        rest = xt - xt.astype(jnp.bfloat16).astype(jnp.float32)
        packed = jnp.where(lanes4 < 2 * size, xt, rest).astype(jnp.bfloat16)
        xtp[b] = packed
        slab_copy(b).wait()
        part = pl.ds(pl.multiple_of(b * blk, blk), blk)
        us_ref[part, :] = us_ref[part, :] - dot(packed, yp[...])

    def line_step(zo, carry):
        update(zo * xn + x)
        return carry

    lax.fori_loop(0, zn, line_step, 0)
    for step in range(1, xn):
        def side_step(zo, carry):
            o = zo * xn + lax.rem(x + step, xn)
            remote(gp.at[o], gp.at[o], side_sem.at[0, 0], panel_sem.at[o], (row, col)).wait_recv()
            prepare(o)
            update(o)
            return carry

        lax.fori_loop(0, zn, side_step, 0)

    @pl.when(row == 0)
    def _():
        us_ref[:size, :] = slab_factor

    own_target.wait()
    for step in range(1, cols_n):
        o = lax.rem(col + step, cols_n)
        remote(t_ref.at[pl.ds(0, tgt)], tg.at[o], t_send.at[0], t_recv.at[o], (row, col)).wait_recv()

    for zo in range(zn):
        @pl.when((z >= zo) & (z + 1 < zn))
        def _():
            up(zo).wait_send()

        @pl.when((z <= zo) & (z > 0))
        def _():
            down(zo).wait_send()

        for step in range(1, xn):
            side(zo, step).wait_send()

    for step in range(1, cols_n):
        target(step).wait_send()

    @pl.when(row == last)
    def _():
        for step in range(1, rows_n):
            slab_panel(step).wait_send()

    @pl.when(first_device)
    def _():
        for c in range(1, cols_n):
            note_out(c).wait_send()

    @pl.when(row == 0)
    def _():
        for step in range(1, rows_n):
            note_on(step).wait_send()


def finish(us_in, tg, xtp, pf_in, zp, z_in, sel, us_out, st_out, pf_out, st, sems):
    count, _, blk = tg.shape
    part_rows = us_in.shape[0] // 4
    copies = []
    for part in range(4):
        rows = pl.ds(part * part_rows, part_rows)
        copies.append(pltpu.make_async_copy(us_in.at[rows], us_out.at[rows], sems.at[part]))
    copies.append(pltpu.make_async_copy(pf_in, pf_out, sems.at[4]))
    for copy in copies:
        copy.start()
    for b in range(count):
        st[:, b * blk : (b + 1) * blk] = tg[b] - dot(zp[...], xtp[b], dims=((1,), (1,)))
    width = z_in.shape[1]
    st[:, :width] = jnp.where(sel[...] > 0.5, z_in[...], st[:, :width])
    copies.append(pltpu.make_async_copy(st, st_out, sems.at[5]))
    copies[-1].start()
    for copy in copies:
        copy.wait()


def body(rows_n, cols_n, kernel_panel, kernel_slab, targets):
    size, blk = kernel_panel.shape
    rows, _ = kernel_slab.shape
    tgt = targets.shape[0] // cols_n
    xn = cols_n // Z_SIZE
    f32, bf16 = jnp.float32, jnp.bfloat16
    hbm = pl.BlockSpec(memory_space=pltpu.HBM)
    vmem = pl.BlockSpec(memory_space=pltpu.VMEM)
    dma = pltpu.SemaphoreType.DMA
    held = pl.pallas_call(
        functools.partial(kernel, rows_n, cols_n),
        out_shape=[
            pltpu.VMEM((rows, blk), f32),
            pltpu.VMEM((cols_n, tgt, blk), f32),
            pltpu.VMEM((cols_n, blk, 4 * size), bf16),
            pltpu.VMEM((size, blk), f32),
            pltpu.VMEM((tgt, 4 * size), bf16),
            pltpu.VMEM((tgt, 2 * size), f32),
            pltpu.VMEM((tgt, 2 * size), f32),
        ],
        in_specs=[hbm] * 3,
        out_specs=[vmem] * 7,
        scratch_shapes=[
            pltpu.VMEM((cols_n, size, blk), f32),
            pltpu.VMEM((size, blk), f32),
            pltpu.VMEM((size, 2 * size), f32),
            pltpu.VMEM((cols_n, size, 2 * size), f32),
            pltpu.VMEM((cols_n * tgt, 2 * size), f32),
            pltpu.VMEM((cols_n, blk, 4 * size), bf16),
            pltpu.VMEM((6 * size, 4 * size), bf16),
            pltpu.VMEM((4 * size, blk), bf16),
            dma((cols_n,)), dma((3,)), dma((Z_SIZE,)), dma((Z_SIZE,)), dma((Z_SIZE, xn - 1)), dma((cols_n,)),
            dma((cols_n - 1,)), dma((cols_n,)), dma((rows_n - 1,)), dma,
            dma((cols_n,)), dma((rows_n - 1,)), dma,
        ],
        compiler_params=pltpu.CompilerParams(
            collective_id=0, has_side_effects=True, vmem_limit_bytes=48 * 1024 * 1024
        ),
        cost_estimate=pl.CostEstimate(
            flops=2 * rows * blk * 4 * size, bytes_accessed=4 * rows * blk, transcendentals=0
        ),
    )(kernel_panel, targets, kernel_slab)
    return pl.pallas_call(
        finish,
        out_shape=[
            jax.ShapeDtypeStruct((rows, blk), f32),
            jax.ShapeDtypeStruct((tgt, rows), f32),
            jax.ShapeDtypeStruct((size, blk), f32),
        ],
        in_specs=[vmem] * 7,
        out_specs=[hbm] * 3,
        scratch_shapes=[pltpu.VMEM((tgt, rows), f32), dma((6,))],
        compiler_params=pltpu.CompilerParams(vmem_limit_bytes=36 * 1024 * 1024),
        cost_estimate=pl.CostEstimate(
            flops=2 * rows * tgt * 4 * size, bytes_accessed=4 * rows * blk, transcendentals=0
        ),
    )(*held)


def solution(mesh):
    in_specs = (P(None, ("row", "col")), P("row", "col"), P(None, ("row", "col")))
    out_specs = (P("row", "col"), P("col", "row"), P(None, ("row", "col")))
    step = functools.partial(body, mesh.shape["row"], mesh.shape["col"])
    return jax.shard_map(step, mesh=mesh, in_specs=in_specs, out_specs=out_specs, check_vma=False)
```

time: 52.4 us -> 42.4 us (0.81)
  the two profiles are of different devices: /device:TPU:0 before, /device:TPU:7 now
where the time goes in v2:
time: 42.4 us; the launch traced here: 42.2 us
  Pallas kernels  41.6 us (98%)
  between operations  0.64 us (2%)
    pallas_call x1, Pallas kernels, body(): pl.pallas_call(functools.partial(kernel, rows_n, cols_n), out_shape=[pltp...  37.5 us
    pallas_call x1, Pallas kernels, body(): pl.pallas_call(finish, out_shape=[jax.ShapeDtypeStruct((rows, blk), f32),...  4.11 us

profile of v2, /device:TPU:7, one launch (start us, length us, event | category | flops | bytes accessed | tf_op | source)
XLA Modules:
  0.0 42.2 jit_solution(12459642090195549599)
XLA Ops:
  0.6 37.5 %shard_map.58 = (f32[4096,512]{1,0:T(8,128)S(1)}, f32[8,32,512]{2,1,0:T(8,128)S(1)}, bf16[8,512,256]{2,1,0:T(8,128)(2,1)S(1)}, f32[64,512]{1,0:T(8,128)S(1)}, bf...) custom-call(f32[64,512]{1,0:T(8,128)} %k_ref.1, f32[256,512]{1,0:T(8,128)} %t_ref.1, ...), custom_call_target="tpu_custom_call" | custom-call | flops 1073741824 | bytes 8388608 | tf_op jit(solution)/shard_map/pallas_call | solution.py:336
  38.1 4.1 %shard_map.59 = (f32[4096,512]{1,0:T(8,128)}, f32[32,4096]{1,0:T(8,128)}, f32[64,512]{1,0:T(8,128)}) custom-call(f32[4096,512]{1,0:T(8,128)S(1)} %get-tuple-element.10.us_in, f32[8,32,512]{2,1,0:T(8,128)S(1)} %get-tuple-element.11.tg, bf16[8,512,256]{2,1,0:T(8,128)(2,1)S(1)} %get-tuple-element.12.xtp, f32[64,512]{1,0:T(8,128)S(1)} %get-tuple-element.13.pf_in, ...), custom_call_target="tpu_custom_call" | custom-call | flops 67108864 | bytes 8388608 | tf_op jit(solution)/shard_map/pallas_call | solution.py:369

commit v3 on v2

--- a/solution.py
+++ b/solution.py
@@ -10,6 +10,8 @@
 MESH = pl.DeviceIdType.MESH
 HIGHEST = lax.Precision.HIGHEST
 Z_SIZE = 4
+PIECES = 2
+EARLY = 16
 
 
 def dot(a, b, dims=((1,), (0,)), precision=None):
@@ -84,20 +86,34 @@
     for b in range(cols_n):
         slab_copy(b).start()
     own_panel.wait()
+
+    @pl.when(first_device)
+    def _():
+        corner = gp[0, :, : 2 * size]
+        rows = lax.broadcasted_iota(jnp.int32, corner.shape, 0)
+        lanes = lax.broadcasted_iota(jnp.int32, corner.shape, 1)
+        work = jnp.where(lanes < size, corner, jnp.where(lanes == rows + size, 1.0, 0.0))
+        for j in range(0, EARLY, 2):
+            work = eliminate_pair(work, j)
+        notes[0] = work
+
     pl.semaphore_wait(barrier, cols_n - 1 + rows_n - 1)
 
-    def up(zo):
+    def piece(o, h):
+        return gp.at[o, pl.ds(h * (size // PIECES), size // PIECES)]
+
+    def up(zo, h):
         o = zo * xn + x
-        return remote(gp.at[o], gp.at[o], up_sem.at[zo], panel_sem.at[o], (row, col + xn))
-
-    def down(zo):
+        return remote(piece(o, h), piece(o, h), up_sem.at[zo, h], panel_sem.at[o, h], (row, col + xn))
+
+    def down(zo, h):
         o = zo * xn + x
-        return remote(gp.at[o], gp.at[o], down_sem.at[zo], panel_sem.at[o], (row, col - xn))
-
-    def side(zo, step):
+        return remote(piece(o, h), piece(o, h), down_sem.at[zo, h], panel_sem.at[o, h], (row, col - xn))
+
+    def side(zo, step, h):
         o = zo * xn + x
         peer = z * xn + lax.rem(x + step, xn)
-        return remote(gp.at[o], gp.at[o], side_sem.at[zo, step - 1], panel_sem.at[o], (row, peer))
+        return remote(piece(o, h), piece(o, h), side_sem.at[zo, step - 1, h], panel_sem.at[o, h], (row, peer))
 
     def slab_panel(step):
         return remote(gp.at[col], ks, ks_send.at[step - 1], ks_recv, (lax.rem(row + step, rows_n), col))
@@ -128,56 +144,75 @@
         lhs[o] = jnp.concatenate([pair, other], axis=1)
 
     def pass_up(d):
-        up(z - d).wait_recv()
-
+        for h in range(PIECES):
+            up(z - d, h).wait_recv()
+
+            @pl.when(z + 1 < zn)
+            def _():
+                up(z - d, h).start()
+
+            for step in range(1, xn):
+                side(z - d, step, h).start()
+
+    def pass_down(d):
+        for h in range(PIECES):
+            down(z + d, h).wait_recv()
+
+            @pl.when(z > 0)
+            def _():
+                down(z + d, h).start()
+
+            for step in range(1, xn):
+                side(z + d, step, h).start()
+
+    def take_side(zo):
+        for step in range(1, xn):
+            o = zo * xn + lax.rem(x + step, xn)
+            for h in range(PIECES):
+                remote(piece(o, h), piece(o, h), side_sem.at[0, 0, 0], panel_sem.at[o, h], (row, col)).wait_recv()
+            prepare(o)
+
+    def take_sides(d):
+        if d == 0:
+            take_side(z)
+        else:
+            @pl.when(z - d >= 0)
+            def _():
+                take_side(z - d)
+
+            @pl.when(z + d < zn)
+            def _():
+                take_side(z + d)
+
+    for h in range(PIECES):
         @pl.when(z + 1 < zn)
         def _():
-            up(z - d).start()
-
-        for step in range(1, xn):
-            side(z - d, step).start()
-
-    def pass_down(d):
-        down(z + d).wait_recv()
+            up(z, h).start()
 
         @pl.when(z > 0)
         def _():
-            down(z + d).start()
+            down(z, h).start()
 
         for step in range(1, xn):
-            side(z + d, step).start()
-
-    @pl.when(z + 1 < zn)
-    def _():
-        up(z).start()
-
-    @pl.when(z > 0)
-    def _():
-        down(z).start()
-
-    for step in range(1, xn):
-        side(z, step).start()
+            side(z, step, h).start()
 
     @pl.when(row == last)
     def _():
         for step in range(1, rows_n):
             slab_panel(step).start()
 
-    for step in range(1, cols_n):
-        target(step).start()
+    sends = list(range(1, cols_n))
+    groups = [sends[g::zn] for g in range(zn)]
 
     @pl.when(first_device)
     def _():
-        corner = gp[0, :, : 2 * size]
-        rows = lax.broadcasted_iota(jnp.int32, corner.shape, 0)
-        lanes = lax.broadcasted_iota(jnp.int32, corner.shape, 1)
-        work = jnp.where(lanes < size, corner, jnp.where(lanes == rows + size, 1.0, 0.0))
-        for j in range(0, size, 2):
+        for step in sends:
+            target(step).start()
+        work = notes[0]
+        for j in range(EARLY, size, 2):
             work = eliminate_pair(work, j)
-            if j == size // 2:
-                pass_down(1)
-            if j == 3 * size // 4:
-                pass_down(2)
+        rows = lax.broadcasted_iota(jnp.int32, work.shape, 0)
+        lanes = lax.broadcasted_iota(jnp.int32, work.shape, 1)
         diagonal = jnp.sum(jnp.where(lanes == rows, work, 0.0), axis=1, keepdims=True)
         done = work * (1.0 / jnp.sqrt(diagonal))
         own_lead.wait()
@@ -189,31 +224,52 @@
         note[...] = notes[0]
         for step in range(1, rows_n):
             note_on(step).start()
-        pass_down(3)
+        for d in range(1, zn):
+            pass_down(d)
         prepare(col)
         for d in range(1, zn):
             prepare(col + d * xn)
+            take_sides(d - 1)
 
     @pl.when(jnp.logical_not(first_device))
     def _():
         prepare(col)
         for d in range(1, zn):
+            for step in groups[d - 1]:
+                target(step).start()
+
             @pl.when(z - d >= 0)
             def _():
                 pass_up(d)
+
+            @pl.when(z + d < zn)
+            def _():
+                pass_down(d)
+
+            @pl.when(z - d >= 0)
+            def _():
                 prepare(col - d * xn)
 
             @pl.when(z + d < zn)
             def _():
-                pass_down(d)
                 prepare(col + d * xn)
 
-        remote(note, note, note_fwd.at[0], note_recv, (row, col)).wait_recv()
+            if d < zn - 1:
+                take_sides(d - 1)
+        for step in groups[zn - 1]:
+            target(step).start()
 
         @pl.when(row == 0)
         def _():
+            remote(note, note, note_fwd.at[0], note_recv, (row, col)).wait_recv()
             for step in range(1, rows_n):
                 note_on(step).start()
+
+        take_sides(zn - 2)
+
+        @pl.when(row > 0)
+        def _():
+            remote(note, note, note_fwd.at[0], note_recv, (row, col)).wait_recv()
 
     @pl.when(row == last)
     def _():
@@ -249,20 +305,12 @@
         part = pl.ds(pl.multiple_of(b * blk, blk), blk)
         us_ref[part, :] = us_ref[part, :] - dot(packed, yp[...])
 
-    def line_step(zo, carry):
-        update(zo * xn + x)
+    def update_step(b, carry):
+        update(b)
         return carry
 
-    lax.fori_loop(0, zn, line_step, 0)
-    for step in range(1, xn):
-        def side_step(zo, carry):
-            o = zo * xn + lax.rem(x + step, xn)
-            remote(gp.at[o], gp.at[o], side_sem.at[0, 0], panel_sem.at[o], (row, col)).wait_recv()
-            prepare(o)
-            update(o)
-            return carry
-
-        lax.fori_loop(0, zn, side_step, 0)
+    take_sides(zn - 1)
+    lax.fori_loop(0, cols_n, update_step, 0)
 
     @pl.when(row == 0)
     def _():
@@ -274,16 +322,17 @@
         remote(t_ref.at[pl.ds(0, tgt)], tg.at[o], t_send.at[0], t_recv.at[o], (row, col)).wait_recv()
 
     for zo in range(zn):
-        @pl.when((z >= zo) & (z + 1 < zn))
-        def _():
-            up(zo).wait_send()
-
-        @pl.when((z <= zo) & (z > 0))
-        def _():
-            down(zo).wait_send()
-
-        for step in range(1, xn):
-            side(zo, step).wait_send()
+        for h in range(PIECES):
+            @pl.when((z >= zo) & (z + 1 < zn))
+            def _():
+                up(zo, h).wait_send()
+
+            @pl.when((z <= zo) & (z > 0))
+            def _():
+                down(zo, h).wait_send()
+
+            for step in range(1, xn):
+                side(zo, step, h).wait_send()
 
     for step in range(1, cols_n):
         target(step).wait_send()
@@ -355,7 +404,8 @@
             pltpu.VMEM((cols_n, blk, 4 * size), bf16),
             pltpu.VMEM((6 * size, 4 * size), bf16),
             pltpu.VMEM((4 * size, blk), bf16),
-            dma((cols_n,)), dma((3,)), dma((Z_SIZE,)), dma((Z_SIZE,)), dma((Z_SIZE, xn - 1)), dma((cols_n,)),
+            dma((cols_n,)), dma((3,)), dma((Z_SIZE, PIECES)), dma((Z_SIZE, PIECES)),
+            dma((Z_SIZE, xn - 1, PIECES)), dma((cols_n, PIECES)),
             dma((cols_n - 1,)), dma((cols_n,)), dma((rows_n - 1,)), dma,
             dma((cols_n,)), dma((rows_n - 1,)), dma,
         ],

time: 42.4 us -> 38.7 us (0.913)
  the two profiles are of different devices: /device:TPU:7 before, /device:TPU:0 now
where the time goes in v3:
time: 38.7 us; the launch traced here: 38.5 us
  Pallas kernels  37.9 us (98%)
  between operations  0.64 us (2%)
    pallas_call x1, Pallas kernels, body(): pl.pallas_call(functools.partial(kernel, rows_n, cols_n), out_shape=[pltp...  33.8 us
    pallas_call x1, Pallas kernels, body(): pl.pallas_call(finish, out_shape=[jax.ShapeDtypeStruct((rows, blk), f32),...  4.11 us

profile of v3, /device:TPU:0, one launch (start us, length us, event | category | flops | bytes accessed | tf_op | source)
XLA Modules:
  0.0 38.5 jit_solution(18262107016671974720)
XLA Ops:
  0.6 33.8 %shard_map.58 = (f32[4096,512]{1,0:T(8,128)S(1)}, f32[8,32,512]{2,1,0:T(8,128)S(1)}, bf16[8,512,256]{2,1,0:T(8,128)(2,1)S(1)}, f32[64,512]{1,0:T(8,128)S(1)}, bf...) custom-call(f32[64,512]{1,0:T(8,128)} %k_ref.1, f32[256,512]{1,0:T(8,128)} %t_ref.1, ...), custom_call_target="tpu_custom_call" | custom-call | flops 1073741824 | bytes 8388608 | tf_op jit(solution)/shard_map/pallas_call | solution.py:385
  34.4 4.1 %shard_map.59 = (f32[4096,512]{1,0:T(8,128)}, f32[32,4096]{1,0:T(8,128)}, f32[64,512]{1,0:T(8,128)}) custom-call(f32[4096,512]{1,0:T(8,128)S(1)} %get-tuple-element.10.us_in, f32[8,32,512]{2,1,0:T(8,128)S(1)} %get-tuple-element.11.tg, bf16[8,512,256]{2,1,0:T(8,128)(2,1)S(1)} %get-tuple-element.12.xtp, f32[64,512]{1,0:T(8,128)S(1)} %get-tuple-element.13.pf_in, ...), custom_call_target="tpu_custom_call" | custom-call | flops 67108864 | bytes 8388608 | tf_op jit(solution)/shard_map/pallas_call | solution.py:419

commit v4 on v3

--- a/solution.py
+++ b/solution.py
@@ -26,24 +26,32 @@
     return high, mid, low
 
 
-def eliminate_pair(work, j):
-    rows = lax.broadcasted_iota(jnp.int32, work.shape, 0)
-    first, second = work[j : j + 1, :], work[j + 1 : j + 2, :]
-    cross = work[j + 1 : j + 2, j : j + 1]
-    scale = 1.0 / work[j : j + 1, j : j + 1]
-    ratio = cross * scale
-    below = second - ratio * first
-    other = 1.0 / (work[j + 1 : j + 2, j + 1 : j + 2] - ratio * cross)
-    second_part = below * other
-    first_part = first * scale - ratio * second_part
-    change = work[:, j : j + 1] * first_part + work[:, j + 1 : j + 2] * second_part
-    return jnp.where(rows > j + 1, work - change, jnp.where(rows == j + 1, below, work))
+def eliminate(work, begin, end):
+    groups = [work[g : g + 8] for g in range(0, begin // 8 * 8, 8)]
+    work = work[begin // 8 * 8 :]
+    for j in range(begin, end, 2):
+        i = j % 8
+        rows = lax.broadcasted_iota(jnp.int32, work.shape, 0)
+        first, second = work[i : i + 1, :], work[i + 1 : i + 2, :]
+        cross = work[i + 1 : i + 2, j : j + 1]
+        scale = 1.0 / work[i : i + 1, j : j + 1]
+        ratio = cross * scale
+        below = second - ratio * first
+        other = 1.0 / (work[i + 1 : i + 2, j + 1 : j + 2] - ratio * cross)
+        second_part = below * other
+        first_part = first * scale - ratio * second_part
+        change = work[:, j : j + 1] * first_part + work[:, j + 1 : j + 2] * second_part
+        work = jnp.where(rows > i + 1, work - change, jnp.where(rows == i + 1, below, work))
+        if i == 6:
+            groups.append(work[:8])
+            work = work[8:]
+    return jnp.concatenate(groups + ([work] if end < groups[0].shape[1] // 2 else []), axis=0)
 
 
 def kernel(
     rows_n, cols_n, k_ref, t_ref, s_ref,
-    us_ref, tg, xtp, pf_ref, zp_ref, z_ref, sel_ref,
-    gp, ks, note, notes, lead, lhs, rhs, yp,
+    us_ref, tg, lhs, note, own_ref, sel_ref,
+    gp, ks, notes, lead, weights,
     slab_sem, own_sem, up_sem, down_sem, side_sem, panel_sem, t_send, t_recv, ks_send, ks_recv,
     note_send, note_fwd, note_recv,
 ):
@@ -93,9 +101,7 @@
         rows = lax.broadcasted_iota(jnp.int32, corner.shape, 0)
         lanes = lax.broadcasted_iota(jnp.int32, corner.shape, 1)
         work = jnp.where(lanes < size, corner, jnp.where(lanes == rows + size, 1.0, 0.0))
-        for j in range(0, EARLY, 2):
-            work = eliminate_pair(work, j)
-        notes[0] = work
+        notes[0] = eliminate(work, 0, EARLY)
 
     pl.semaphore_wait(barrier, cols_n - 1 + rows_n - 1)
 
@@ -208,9 +214,7 @@
     def _():
         for step in sends:
             target(step).start()
-        work = notes[0]
-        for j in range(EARLY, size, 2):
-            work = eliminate_pair(work, j)
+        work = eliminate(notes[0], EARLY, size)
         rows = lax.broadcasted_iota(jnp.int32, work.shape, 0)
         lanes = lax.broadcasted_iota(jnp.int32, work.shape, 1)
         diagonal = jnp.sum(jnp.where(lanes == rows, work, 0.0), axis=1, keepdims=True)
@@ -279,38 +283,21 @@
     def _():
         remote(gp.at[col], ks, ks_send.at[0], ks_recv, (row, col)).wait_recv()
 
-    inverse = note[:, size:]
-    wide = jnp.concatenate([note[...]] * 4, axis=0).T[size:, :]
-    high, mid, low = split3(wide)
-    rhs[...] = jnp.concatenate([high, high, high, mid, low, mid], axis=0)
-    pf_ref[...] = dot(inverse, gp[col], precision=HIGHEST)
-    slab_factor = dot(inverse, ks[...], precision=HIGHEST)
-    high, mid, _ = split3(slab_factor)
-    yp[...] = jnp.concatenate([high, mid, high, mid], axis=0)
-    solved = dot(note[:tgt, :size], wide, precision=HIGHEST)
-    lanes = lax.broadcasted_iota(jnp.int32, solved.shape, 1)
-    rest = solved - solved.astype(jnp.bfloat16).astype(jnp.float32)
-    zp_ref[...] = jnp.where(lax.rem(lanes, 2 * size) < size, solved, rest).astype(jnp.bfloat16)
-    z_ref[...] = solved[:, : 2 * size]
-    sel_ref[...] = jnp.where((lanes[:, : 2 * size] < size) & (row == 0), 1.0, 0.0)
-
-    lanes4 = lax.broadcasted_iota(jnp.int32, (blk, 4 * size), 1)
-
-    def update(b):
-        xt = dot(lhs[b], rhs[: 4 * size]) + dot(lhs[b, :, : 2 * size], rhs[4 * size :])
-        rest = xt - xt.astype(jnp.bfloat16).astype(jnp.float32)
-        packed = jnp.where(lanes4 < 2 * size, xt, rest).astype(jnp.bfloat16)
-        xtp[b] = packed
+    own_ref[...] = gp[col]
+    lanes = lax.broadcasted_iota(jnp.int32, sel_ref.shape, 1)
+    sel_ref[...] = jnp.where((lanes < size) & (row == 0), 1.0, 0.0)
+    slab_factor = dot(note[:, size:], ks[...], precision=HIGHEST)
+    turned = jnp.concatenate([note[...]] * 2, axis=0).T[size:, :size]
+    high, mid, low = split3(dot(turned, slab_factor, precision=HIGHEST))
+    weights[...] = jnp.concatenate([high, high, high, mid, low, mid], axis=0)
+    for b in range(cols_n):
         slab_copy(b).wait()
-        part = pl.ds(pl.multiple_of(b * blk, blk), blk)
-        us_ref[part, :] = us_ref[part, :] - dot(packed, yp[...])
-
-    def update_step(b, carry):
-        update(b)
-        return carry
 
     take_sides(zn - 1)
-    lax.fori_loop(0, cols_n, update_step, 0)
+    for b in range(cols_n):
+        part = slice(b * blk, (b + 1) * blk)
+        product = dot(lhs[b], weights[: 4 * size]) + dot(lhs[b, :, : 2 * size], weights[4 * size :])
+        us_ref[part, :] = us_ref[part, :] - product
 
     @pl.when(row == 0)
     def _():
@@ -353,20 +340,30 @@
             note_on(step).wait_send()
 
 
-def finish(us_in, tg, xtp, pf_in, zp, z_in, sel, us_out, st_out, pf_out, st, sems):
-    count, _, blk = tg.shape
+def finish(us_in, tg, lhs, note, own, sel, us_out, st_out, pf_out, st, pf, sems):
+    count, tgt, blk = tg.shape
+    size = own.shape[0]
     part_rows = us_in.shape[0] // 4
     copies = []
     for part in range(4):
         rows = pl.ds(part * part_rows, part_rows)
         copies.append(pltpu.make_async_copy(us_in.at[rows], us_out.at[rows], sems.at[part]))
-    copies.append(pltpu.make_async_copy(pf_in, pf_out, sems.at[4]))
     for copy in copies:
         copy.start()
+    inverse = note[:, size:]
+    pf[...] = dot(inverse, own[...], precision=HIGHEST)
+    copies.append(pltpu.make_async_copy(pf, pf_out, sems.at[4]))
+    copies[-1].start()
+    solved = dot(note[:tgt, :size], inverse, dims=((1,), (1,)), precision=HIGHEST)
+    repeated = jnp.concatenate([inverse] * 4, axis=1)
+    high, mid, low = (v.astype(jnp.float32) for v in split3(dot(solved, repeated, precision=HIGHEST)))
+    lanes = lax.broadcasted_iota(jnp.int32, high.shape, 1)
+    front = jnp.where(lanes < 3 * size, high, mid).astype(jnp.bfloat16)
+    back = jnp.where(lanes < size, low, mid)[:, : 2 * size].astype(jnp.bfloat16)
     for b in range(count):
-        st[:, b * blk : (b + 1) * blk] = tg[b] - dot(zp[...], xtp[b], dims=((1,), (1,)))
-    width = z_in.shape[1]
-    st[:, :width] = jnp.where(sel[...] > 0.5, z_in[...], st[:, :width])
+        product = dot(front, lhs[b], dims=((1,), (1,))) + dot(back, lhs[b, :, : 2 * size], dims=((1,), (1,)))
+        st[:, b * blk : (b + 1) * blk] = tg[b] - product
+    st[:, :size] = jnp.where(sel[:, :size] > 0.5, solved, st[:, :size])
     copies.append(pltpu.make_async_copy(st, st_out, sems.at[5]))
     copies[-1].start()
     for copy in copies:
@@ -388,22 +385,18 @@
             pltpu.VMEM((rows, blk), f32),
             pltpu.VMEM((cols_n, tgt, blk), f32),
             pltpu.VMEM((cols_n, blk, 4 * size), bf16),
+            pltpu.VMEM((size, 2 * size), f32),
             pltpu.VMEM((size, blk), f32),
-            pltpu.VMEM((tgt, 4 * size), bf16),
-            pltpu.VMEM((tgt, 2 * size), f32),
             pltpu.VMEM((tgt, 2 * size), f32),
         ],
         in_specs=[hbm] * 3,
-        out_specs=[vmem] * 7,
+        out_specs=[vmem] * 6,
         scratch_shapes=[
             pltpu.VMEM((cols_n, size, blk), f32),
             pltpu.VMEM((size, blk), f32),
-            pltpu.VMEM((size, 2 * size), f32),
             pltpu.VMEM((cols_n, size, 2 * size), f32),
             pltpu.VMEM((cols_n * tgt, 2 * size), f32),
-            pltpu.VMEM((cols_n, blk, 4 * size), bf16),
-            pltpu.VMEM((6 * size, 4 * size), bf16),
-            pltpu.VMEM((4 * size, blk), bf16),
+            pltpu.VMEM((6 * size, blk), bf16),
             dma((cols_n,)), dma((3,)), dma((Z_SIZE, PIECES)), dma((Z_SIZE, PIECES)),
             dma((Z_SIZE, xn - 1, PIECES)), dma((cols_n, PIECES)),
             dma((cols_n - 1,)), dma((cols_n,)), dma((rows_n - 1,)), dma,
@@ -413,7 +406,7 @@
             collective_id=0, has_side_effects=True, vmem_limit_bytes=48 * 1024 * 1024
         ),
         cost_estimate=pl.CostEstimate(
-            flops=2 * rows * blk * 4 * size, bytes_accessed=4 * rows * blk, transcendentals=0
+            flops=2 * rows * blk * 6 * size, bytes_accessed=4 * rows * blk, transcendentals=0
         ),
     )(kernel_panel, targets, kernel_slab)
     return pl.pallas_call(
@@ -423,9 +416,9 @@
             jax.ShapeDtypeStruct((tgt, rows), f32),
             jax.ShapeDtypeStruct((size, blk), f32),
         ],
-        in_specs=[vmem] * 7,
+        in_specs=[vmem] * 6,
         out_specs=[hbm] * 3,
-        scratch_shapes=[pltpu.VMEM((tgt, rows), f32), dma((6,))],
+        scratch_shapes=[pltpu.VMEM((tgt, rows), f32), pltpu.VMEM((size, blk), f32), dma((6,))],
         compiler_params=pltpu.CompilerParams(vmem_limit_bytes=36 * 1024 * 1024),
         cost_estimate=pl.CostEstimate(
             flops=2 * rows * tgt * 4 * size, bytes_accessed=4 * rows * blk, transcendentals=0

time: 38.7 us -> 34.6 us (0.89)
  Pallas kernels: 37.9 us -> 33.8 us
    pallas_call x1, Pallas kernels: 33.8 us -> 29.5 us  [body(): pl.pallas_call(functools.partial(kernel, rows_n, cols_n), out_shape=[pltp...]
where the time goes in v4:
time: 34.6 us; the launch traced here: 34.4 us
  Pallas kernels  33.8 us (98%)
  between operations  0.64 us (2%)
    pallas_call x1, Pallas kernels, body(): pl.pallas_call(functools.partial(kernel, rows_n, cols_n), out_shape=[pltp...  29.5 us
    pallas_call x1, Pallas kernels, body(): pl.pallas_call(finish, out_shape=[jax.ShapeDtypeStruct((rows, blk), f32),...  4.3 us

profile of v4, /device:TPU:0, one launch (start us, length us, event | category | flops | bytes accessed | tf_op | source)
XLA Modules:
  0.0 34.4 jit_solution(1502055447249392451)
XLA Ops:
  0.6 29.5 %shard_map.58 = (f32[4096,512]{1,0:T(8,128)S(1)}, f32[8,32,512]{2,1,0:T(8,128)S(1)}, bf16[8,512,256]{2,1,0:T(8,128)(2,1)S(1)}, f32[64,128]{1,0:T(8,128)S(1)}, f3...) custom-call(f32[64,512]{1,0:T(8,128)} %k_ref.1, f32[256,512]{1,0:T(8,128)} %t_ref.1, f32[4096,512]{1,0:T(8,128)} %s_ref.1), custom_call_target="tpu_custom_call" | custom-call | flops 1610612736 | bytes 8388608 | tf_op jit(solution)/shard_map/pallas_call | solution.py:382
  30.1 4.3 %shard_map.59 = (f32[4096,512]{1,0:T(8,128)}, f32[32,4096]{1,0:T(8,128)}, f32[64,512]{1,0:T(8,128)}) custom-call(f32[4096,512]{1,0:T(8,128)S(1)} %get-tuple-element.9.us_in, f32[8,32,512]{2,1,0:T(8,128)S(1)} %get-tuple-element.10.tg, bf16[8,512,256]{2,1,0:T(8,128)(2,1)S(1)} %get-tuple-element.11.lhs, f32[64,128]{1,0:T(8,128)S(1)} %get-tuple-element.12.note, ...), custom_call_target="tpu_custom_call" | custom-call | flops 67108864 | bytes 8388608 | tf_op jit(solution)/shard_map/pallas_call | solution.py:412

commit v5 on v4

--- a/solution.py
+++ b/solution.py
@@ -11,7 +11,7 @@
 HIGHEST = lax.Precision.HIGHEST
 Z_SIZE = 4
 PIECES = 2
-EARLY = 16
+EARLY = 40
 
 
 def dot(a, b, dims=((1,), (0,)), precision=None):
@@ -212,8 +212,6 @@
 
     @pl.when(first_device)
     def _():
-        for step in sends:
-            target(step).start()
         work = eliminate(notes[0], EARLY, size)
         rows = lax.broadcasted_iota(jnp.int32, work.shape, 0)
         lanes = lax.broadcasted_iota(jnp.int32, work.shape, 1)
@@ -230,6 +228,8 @@
             note_on(step).start()
         for d in range(1, zn):
             pass_down(d)
+        for step in sends:
+            target(step).start()
         prepare(col)
         for d in range(1, zn):
             prepare(col + d * xn)

time: 34.6 us -> 34.1 us (0.986)
  Pallas kernels: 33.8 us -> 33.3 us
    pallas_call x1, Pallas kernels: 29.5 us -> 29 us  [body(): pl.pallas_call(functools.partial(kernel, rows_n, cols_n), out_shape=[pltp...]
where the time goes in v5:
time: 34.1 us; the launch traced here: 33.9 us
  Pallas kernels  33.3 us (98%)
  between operations  0.64 us (2%)
    pallas_call x1, Pallas kernels, body(): pl.pallas_call(functools.partial(kernel, rows_n, cols_n), out_shape=[pltp...  29 us
    pallas_call x1, Pallas kernels, body(): pl.pallas_call(finish, out_shape=[jax.ShapeDtypeStruct((rows, blk), f32),...  4.3 us

profile of v5, /device:TPU:0, one launch (start us, length us, event | category | flops | bytes accessed | tf_op | source)
XLA Modules:
  0.0 33.9 jit_solution(17873684677947805194)
XLA Ops:
  0.6 29.0 %shard_map.58 = (f32[4096,512]{1,0:T(8,128)S(1)}, f32[8,32,512]{2,1,0:T(8,128)S(1)}, bf16[8,512,256]{2,1,0:T(8,128)(2,1)S(1)}, f32[64,128]{1,0:T(8,128)S(1)}, f3...) custom-call(f32[64,512]{1,0:T(8,128)} %k_ref.1, f32[256,512]{1,0:T(8,128)} %t_ref.1, f32[4096,512]{1,0:T(8,128)} %s_ref.1), custom_call_target="tpu_custom_call" | custom-call | flops 1610612736 | bytes 8388608 | tf_op jit(solution)/shard_map/pallas_call | solution.py:382
  29.6 4.3 %shard_map.59 = (f32[4096,512]{1,0:T(8,128)}, f32[32,4096]{1,0:T(8,128)}, f32[64,512]{1,0:T(8,128)}) custom-call(f32[4096,512]{1,0:T(8,128)S(1)} %get-tuple-element.9.us_in, f32[8,32,512]{2,1,0:T(8,128)S(1)} %get-tuple-element.10.tg, bf16[8,512,256]{2,1,0:T(8,128)(2,1)S(1)} %get-tuple-element.11.lhs, f32[64,128]{1,0:T(8,128)S(1)} %get-tuple-element.12.note, ...), custom_call_target="tpu_custom_call" | custom-call | flops 67108864 | bytes 8388608 | tf_op jit(solution)/shard_map/pallas_call | solution.py:412
